TPU v7x, 32 devices: a whole 2x2x4 slice. The times are simulated.
32 devices in a mesh: band: 8 (over y, x, core), grid: 4 (over z).
Axes of the slice: x: 2, y: 2, z: 4, core: 2. Of those that a mesh axis runs over, the one named last changes fastest.
Arguments:
- orbitals: float32 [32, 48, 2304], P('band', 'grid'), may hold values from -5.5 to 6.6
- occupation: int32 [32], P('band'), may hold values from 0 to 2
- cutoff: int32 [], replicated, may hold values from 144 to 1728
Outputs:
- exchange_term: float32 [32, 48, 2304], P('band', 'grid')
All inputs are finite; a program needn't handle non-finite values.
Results may differ from a plain program's by a relative error of at most 0.00005.
Values sent between devices are 32-bit elements; how exact they have to be, the bound alone decides.
A program may use at most 128 MiB of HBM per device.

v0:
```python
import jax
import jax.numpy as jnp
from jax import lax
from jax.sharding import PartitionSpec as P

G = 48


screen_alpha = 2.0
screen_scale = 4.0


def shifted(block, axis, distance):
    devices = range(lax.axis_size(axis))
    route = [((i - distance) % len(devices), i) for i in devices]
    return lax.ppermute(block, axis, route)


def transform_tables(extent, cutoff):
    position = jnp.arange(extent, dtype=jnp.int32)
    middle = extent // 2
    frequency = jnp.where(position <= middle, position, position - middle)
    phase_index = frequency[:, None] * position[None, :] % extent
    angles = 2.0 * jnp.pi / extent * phase_index.astype(jnp.float32)
    transform = jnp.where((position <= middle)[:, None], jnp.cos(angles), jnp.sin(angles))
    weight = jnp.where((position == 0) | (position == middle), 1.0, 2.0).astype(jnp.float32)
    shells = (
        frequency[:, None, None] ** 2
        + frequency[None, :, None] ** 2
        + frequency[None, None, :] ** 2
    )
    ratios = shells.astype(jnp.float32) / screen_alpha
    screen = jnp.where(
        shells > 0, (1.0 - jnp.exp(-ratios)) / jnp.maximum(ratios, 1.0 / screen_alpha), 1.0
    )
    factor = weight[:, None, None] * weight[None, :, None] * weight[None, None, :]
    kernel = jnp.where(shells <= cutoff, screen_scale * screen * factor / float(extent**3), 0.0)
    return (transform, kernel.reshape(extent, extent * extent))


def apply_transform(matrix, fields):
    batch_size, extent, row_cells = fields.shape
    first = jnp.matmul(matrix, fields, precision=lax.Precision.HIGHEST)
    second = jnp.matmul(
        matrix, first.reshape(batch_size * extent, extent, extent), precision=lax.Precision.HIGHEST
    )
    third = jnp.matmul(
        second.reshape(batch_size * extent * extent, extent),
        matrix.T,
        precision=lax.Precision.HIGHEST,
    )
    return third.reshape(batch_size, extent, row_cells)


def screened_potential(fields, transform, kernel):
    spectrum = apply_transform(transform, fields) * kernel[None]
    return apply_transform(transform.T, spectrum)


def solve_pairs(densities, transform, kernel):
    groups = lax.axis_size("grid")
    pair_count, planes, row_cells = densities.shape
    shaped = densities.reshape(groups, pair_count // groups, planes, row_cells)
    pieces = lax.all_to_all(shaped, "grid", split_axis=0, concat_axis=2, tiled=True)
    fields = pieces.reshape(pieces.shape[1], pieces.shape[2], pieces.shape[3])
    potential = screened_potential(fields, transform, kernel).reshape(pieces.shape)
    sliced = lax.all_to_all(potential, "grid", split_axis=2, concat_axis=0, tiled=True)
    return sliced.reshape(pair_count, planes, row_cells)


def pair_densities(home_orbitals, visitor_orbitals):
    orbital_count, planes, row_cells = home_orbitals.shape
    products = home_orbitals[:, None] * visitor_orbitals[None, :]
    return products.reshape(orbital_count * orbital_count, planes, row_cells)


def pair_terms(home_orbitals, home_weights, visitor_orbitals, visitor_weights, potentials):
    orbital_count, planes, row_cells = home_orbitals.shape
    shaped = potentials.reshape(orbital_count, orbital_count, planes, row_cells)
    scaled_visitor = visitor_weights[:, None, None] * visitor_orbitals
    scaled_home = home_weights[:, None, None] * home_orbitals
    to_home = jnp.sum(scaled_visitor[None] * shaped, axis=1)
    to_visitor = jnp.sum(scaled_home[:, None] * shaped, axis=0)
    return (to_home, to_visitor)


def on_device(orbitals, occupation, cutoff):
    transform, kernel = transform_tables(G, cutoff)
    weights = occupation.astype(jnp.float32) * 0.5
    half_cycle = lax.axis_size("band") // 2
    potentials = solve_pairs(pair_densities(orbitals, orbitals), transform, kernel)
    applied, unused = pair_terms(orbitals, weights, orbitals, weights, potentials)
    visitor = (orbitals, weights)
    carried = jnp.zeros_like(orbitals)
    for distance in range(1, half_cycle + 1):
        visitor = shifted((visitor[0], visitor[1]), "band", 1)
        potentials = solve_pairs(pair_densities(orbitals, visitor[0]), transform, kernel)
        to_home, to_visitor = pair_terms(orbitals, weights, visitor[0], visitor[1], potentials)
        applied = applied + to_home
        if distance == 1:
            carried = to_visitor
        elif distance < half_cycle:
            carried = shifted(carried, "band", 1) + to_visitor
    applied = applied + shifted(carried, "band", 1 - half_cycle)
    return -applied


def solution(mesh):
    placed = (P("band", "grid", None), P("band"), P())
    return jax.shard_map(
        on_device, mesh=mesh, in_specs=placed, out_specs=P("band", "grid", None), check_vma=False
    )
```

profile of v0, /device:TPU:11, one launch (start us, length us, event | category | flops | bytes accessed | tf_op | source)
XLA Modules:
  0.0 716.6 jit_solution(702701015265867986)
XLA Ops:
  1.8 5.6 collective-permute-done.1
  10.6 5.2 collective-permute-done.3
  19.2 5.2 collective-permute-done.5
  37.6 44.1 %all_to_all.165 = f32[4,4,12,2304]{3,1,2,0:T(4,128)S(1)} all-to-all(f32[4,4,12,2304]{3,1,2,0:T(4,128)S(1)} %get-tuple-element.12), channel_id=1, replica_groups=mesh['band'=8,'grid'=4] {'grid'}, dimensions={0} | all-to-all | bytes 3538944 | tf_op jit(solution)/shard_map/all_to_all | solution.py:64
  81.6 44.2 %all_to_all.166 = f32[4,4,12,2304]{3,1,2,0:T(4,128)} all-to-all(f32[4,4,12,2304]{3,1,2,0:T(4,128)S(1)} %get-tuple-element.13), channel_id=1, replica_groups=mesh['band'=8,'grid'=4] {'grid'}, dimensions={0} | all-to-all | bytes 3538944 | tf_op jit(solution)/shard_map/all_to_all | solution.py:64
  125.8 43.6 %all_to_all.167 = f32[4,4,12,2304]{3,1,2,0:T(4,128)} all-to-all(f32[4,4,12,2304]{3,1,2,0:T(4,128)S(1)} %get-tuple-element.14), channel_id=1, replica_groups=mesh['band'=8,'grid'=4] {'grid'}, dimensions={0} | all-to-all | bytes 3538944 | tf_op jit(solution)/shard_map/all_to_all | solution.py:64
  169.4 5.2 all-to-all-start.8
  187.3 24.1 %all-to-all-done.8 = f32[4,4,12,2304]{3,1,2,0:T(4,128)S(1)} async-done(((f32[4,4,12,2304]{3,1,2,0:T(4,128)}), f32[4,4,12,2304]{3,1,2,0:T(4,128)S(1)}, u32[]{:S(2)}, u32[]{:S(2)}) %all-to-all-start.8) | async-done | bytes 1769504 | tf_op jit(solution)/shard_map/all_to_all | solution.py:64
  212.6 8.6 %all-to-all-start = ((f32[4,4,12,2304]{3,1,2,0:T(4,128)}), f32[4,4,12,2304]{3,1,2,0:T(4,128)}, u32[]{:S(2)}, u32[]{:S(2)}) async-start(f32[4,4,12,2304]{3,1,2,0:T(4,128)} %get-tuple-element.11), calls=%async_computation | async-start | bytes 3538944 | tf_op jit(solution)/shard_map/all_to_all | solution.py:64
  225.7 5.7 reshape.300
  245.0 5.1 reshape.301
  250.1 9.2 %fusion.43 = f32[9216,48]{1,0:T(8,128)} fusion(f32[9216,48]{0,1:T(8,128)S(1)} %reshape.301, s32[48]{0:T(128)S(1)} %add_select_fusion.1, pred[48]{0:T(512)(128)(4,1)S(1)} %iota_compare_fusion), kind=kOutput, calls=%fused_computation.88 | convolution fusion | flops 254827008 | bytes 3539184 | tf_op jit(solution)/shard_map/dot_general | solution.py:47
  266.9 5.7 reshape.303
  286.2 5.1 reshape.304
  291.3 9.2 %fusion.42 = f32[9216,48]{1,0:T(8,128)} fusion(f32[9216,48]{0,1:T(8,128)S(1)} %reshape.304, s32[48]{0:T(128)S(1)} %add_select_fusion.1, pred[48]{0:T(512)(128)(4,1)S(1)} %iota_compare_fusion), kind=kOutput, calls=%fused_computation.87 | convolution fusion | flops 254827008 | bytes 3539184 | tf_op jit(solution)/shard_map/dot_general | solution.py:47
  315.0 5.7 reshape.306
  339.4 9.2 %fusion.50 = f32[9216,48]{1,0:T(8,128)} fusion(f32[9216,48]{0,1:T(8,128)S(1)} %reshape.307, s32[48]{0:T(128)S(1)} %add_select_fusion.1, pred[48]{0:T(512)(128)(4,1)S(1)} %iota_compare_fusion), kind=kOutput, calls=%fused_computation.95 | convolution fusion | flops 254827008 | bytes 3539184 | tf_op jit(solution)/shard_map/dot_general | solution.py:47
  355.9 5.7 reshape.309
  380.3 9.6 %fusion.45 = f32[9216,48]{1,0:T(8,128)} fusion(f32[9216,48]{0,1:T(8,128)S(1)} %reshape.310, s32[48]{0:T(128)S(1)} %add_select_fusion.1, pred[48]{0:T(512)(128)(4,1)S(1)} %iota_compare_fusion), kind=kOutput, calls=%fused_computation.90 | convolution fusion | flops 254827008 | bytes 3539184 | tf_op jit(solution)/shard_map/dot_general | solution.py:47
  404.1 5.8 reshape.312
  423.6 5.1 reshape.313
  428.7 9.2 %fusion.49 = f32[9216,48]{1,0:T(8,128)} fusion(f32[9216,48]{0,1:T(8,128)S(1)} %reshape.313, s32[48]{0:T(128)S(1)} %add_select_fusion.1, pred[48]{0:T(512)(128)(4,1)S(1)} %iota_compare_fusion), kind=kOutput, calls=%fused_computation.94 | convolution fusion | flops 254827008 | bytes 3539184 | tf_op jit(solution)/shard_map/dot_general | solution.py:47
  445.4 5.7 reshape.315
  469.8 9.2 %fusion.41 = f32[9216,48]{1,0:T(8,128)} fusion(f32[9216,48]{0,1:T(8,128)S(1)} %reshape.316, s32[48]{0:T(128)S(1)} %add_select_fusion.1, pred[48]{0:T(512)(128)(4,1)S(1)} %iota_compare_fusion), kind=kOutput, calls=%fused_computation.86 | convolution fusion | flops 254827008 | bytes 3539184 | tf_op jit(solution)/shard_map/dot_general | solution.py:47
  522.9 9.2 %fusion.48 = f32[9216,48]{1,0:T(8,128)} fusion(f32[9216,48]{0,1:T(8,128)S(1)} %reshape.295, s32[48]{0:T(128)S(1)} %add_select_fusion.1, pred[48]{0:T(512)(128)(4,1)S(1)} %iota_compare_fusion), kind=kOutput, calls=%fused_computation.93 | convolution fusion | flops 254827008 | bytes 3539184 | tf_op jit(solution)/shard_map/dot_general | solution.py:47
  539.7 5.7 reshape.297
  564.1 9.2 %fusion.46 = f32[9216,48]{1,0:T(8,128)} fusion(f32[9216,48]{0,1:T(8,128)S(1)} %reshape.298, s32[48]{0:T(128)S(1)} %add_select_fusion.1, pred[48]{0:T(512)(128)(4,1)S(1)} %iota_compare_fusion), kind=kOutput, calls=%fused_computation.91 | convolution fusion | flops 254827008 | bytes 3539184 | tf_op jit(solution)/shard_map/dot_general | solution.py:47
  588.6 5.7 reshape.318
  613.0 9.2 %fusion.44 = f32[9216,48]{1,0:T(8,128)} fusion(f32[9216,48]{0,1:T(8,128)S(1)} %reshape.319, s32[48]{0:T(128)S(1)} %add_select_fusion.1, pred[48]{0:T(512)(128)(4,1)S(1)} %iota_compare_fusion), kind=kOutput, calls=%fused_computation.89 | convolution fusion | flops 254827008 | bytes 3539184 | tf_op jit(solution)/shard_map/dot_general | solution.py:47
  629.5 5.7 reshape.321
  653.9 9.4 %fusion.47 = f32[9216,48]{1,0:T(8,128)} fusion(f32[9216,48]{0,1:T(8,128)S(1)} %reshape.322, s32[48]{0:T(128)S(1)} %add_select_fusion.1, pred[48]{0:T(512)(128)(4,1)S(1)} %iota_compare_fusion), kind=kOutput, calls=%fused_computation.92 | convolution fusion | flops 254827008 | bytes 3539184 | tf_op jit(solution)/shard_map/dot_general | solution.py:47
  676.0 7.7 %multiply_reduce_fusion.4 = (f32[4,12,2304]{2,1,0:T(8,128)}, f32[4,12,2304]{2,0,1:T(4,128)S(1)}, f32[4,12,2304]{2,0,1:T(4,128)S(1)}, f32[4,12,2304]{2,1,0:T(8,12...) fusion(f32[4,4,12,2304]{3,1,2,0:T(4,128)} %bitcast.48, f32[4,12,2304]{2,0,1:T(4,128)S(1)} %broadcast_multiply_fusion.6, ...), kind=kLoop, calls=%fused_computation.20 | loop fusion | flops 4644864 | bytes 9732096 | tf_op jit(solution)/shard_map/reduce_sum | solution.py:82
  (161 shorter events, 362.6 us)
Async XLA Ops:
  0.0 7.3 %collective-permute-start.1 = (f32[4,12,2304]{2,0,1:T(4,128)}, f32[4,12,2304]{2,0,1:T(4,128)S(1)}, u32[]{:S(2)}, u32[]{:S(2)}) collective-permute-start(f32[4,12,2304]{2,0,1:T(4,128)} %param.3), channel_id=1, source_target_pairs={{28,0},{0,4},{4,8},{8,12},{12,16},{16,20},{20,24},{24,28},{29,1},{... | collective-permute-start | bytes 1327112 | tf_op jit(solution)/shard_map/ppermute | solution.py:16
  7.3 30.2 %copy-start.15 = (f32[4,12,2304]{2,0,1:T(4,128)}, f32[4,12,2304]{2,0,1:T(4,128)S(1)}, u32[]{:S(2)}) copy-start(f32[4,12,2304]{2,0,1:T(4,128)S(1)} %collective-permute-done.1) | copy-start | bytes 1327108
  7.3 8.5 %collective-permute-start.3 = (f32[4,12,2304]{2,0,1:T(4,128)S(1)}, f32[4,12,2304]{2,0,1:T(4,128)S(1)}, u32[]{:S(2)}, u32[]{:S(2)}) collective-permute-start(f32[4,12,2304]{2,0,1:T(4,128)S(1)} %collective-permute-done.1), channel_id=1, source_target_pairs={{28,0},{0,4},{4,8},{8,12},{12,16},{16,20},{20,24},{24,28},{29,1},{... | collective-permute-start | bytes 1327112 | tf_op jit(solution)/shard_map/ppermute | solution.py:16
  15.9 21.7 %copy-start.12 = (f32[4,12,2304]{2,0,1:T(4,128)}, f32[4,12,2304]{2,0,1:T(4,128)S(1)}, u32[]{:S(2)}) copy-start(f32[4,12,2304]{2,0,1:T(4,128)S(1)} %collective-permute-done.3) | copy-start | bytes 1327108
  15.9 8.6 %collective-permute-start.5 = (f32[4,12,2304]{2,0,1:T(4,128)S(1)}, f32[4,12,2304]{2,0,1:T(4,128)S(1)}, u32[]{:S(2)}, u32[]{:S(2)}) collective-permute-start(f32[4,12,2304]{2,0,1:T(4,128)S(1)} %collective-permute-done.3), channel_id=1, source_target_pairs={{28,0},{0,4},{4,8},{8,12},{12,16},{16,20},{20,24},{24,28},{29,1},{... | collective-permute-start | bytes 1327112 | tf_op jit(solution)/shard_map/ppermute | solution.py:16
  24.5 13.1 %copy-start.14 = (f32[4,12,2304]{2,0,1:T(4,128)}, f32[4,12,2304]{2,0,1:T(4,128)S(1)}, u32[]{:S(2)}) copy-start(f32[4,12,2304]{2,0,1:T(4,128)S(1)} %collective-permute-done.5) | copy-start | bytes 1327108
  24.5 8.6 %collective-permute-start.7 = (f32[4,12,2304]{2,0,1:T(4,128)S(1)}, f32[4,12,2304]{2,0,1:T(4,128)S(1)}, u32[]{:S(2)}, u32[]{:S(2)}) collective-permute-start(f32[4,12,2304]{2,0,1:T(4,128)S(1)} %collective-permute-done.5), channel_id=1, source_target_pairs={{28,0},{0,4},{4,8},{8,12},{12,16},{16,20},{20,24},{24,28},{29,1},{... | collective-permute-start | bytes 1327112 | tf_op jit(solution)/shard_map/ppermute | solution.py:16
  169.4 41.9 %all-to-all-start.8 = ((f32[4,4,12,2304]{3,1,2,0:T(4,128)}), f32[4,4,12,2304]{3,1,2,0:T(4,128)S(1)}, u32[]{:S(2)}, u32[]{:S(2)}) async-start(f32[4,4,12,2304]{3,1,2,0:T(4,128)} %get-tuple-element.15), calls=%async_computation.8 | async-start | bytes 3538944 | tf_op jit(solution)/shard_map/all_to_all | solution.py:64
  212.6 94.5 %all-to-all-start = ((f32[4,4,12,2304]{3,1,2,0:T(4,128)}), f32[4,4,12,2304]{3,1,2,0:T(4,128)}, u32[]{:S(2)}, u32[]{:S(2)}) async-start(f32[4,4,12,2304]{3,1,2,0:T(4,128)} %get-tuple-element.11), calls=%async_computation | async-start | bytes 3538944 | tf_op jit(solution)/shard_map/all_to_all | solution.py:64
  307.0 4.9 copy-start.3
  307.0 89.3 %all-to-all-start.3 = ((f32[1,4,48,2304]{3,1,0,2:T(4,128)}), f32[1,4,48,2304]{3,1,0,2:T(4,128)}, u32[]{:S(2)}, u32[]{:S(2)}) async-start(f32[1,4,48,2304]{3,1,0,2:T(4,128)} %copy.161), calls=%async_computation.3 | async-start | bytes 3538944 | tf_op jit(solution)/shard_map/all_to_all | solution.py:67
  396.4 4.7 copy-start.18
  396.4 4.7 copy-start.2
  396.4 89.3 %all-to-all-start.5 = ((f32[1,4,48,2304]{3,1,0,2:T(4,128)}), f32[1,4,48,2304]{3,1,0,2:T(4,128)}, u32[]{:S(2)}, u32[]{:S(2)}) async-start(f32[1,4,48,2304]{3,1,0,2:T(4,128)} %copy.171), calls=%async_computation.5 | async-start | bytes 3538944 | tf_op jit(solution)/shard_map/all_to_all | solution.py:67
  401.1 90.3 %collective-permute-start = (f32[4]{0:T(128)S(1)}, f32[4]{0:T(128)S(1)}, u32[]{:S(2)}, u32[]{:S(2)}) collective-permute-start(f32[4]{0:T(128)S(1)} %convert_multiply_fusion), channel_id=1, source_target_pairs={{28,0},{0,4},{4,8},{8,12},{12,16},{16,20},{20,24},{24,28},{29,1},{... | collective-permute-start | bytes 56 | tf_op jit(solution)/shard_map/ppermute | solution.py:16
  485.7 4.7 copy-start.4
  485.7 94.1 %all-to-all-start.7 = ((f32[1,4,48,2304]{3,1,0,2:T(4,128)}), f32[1,4,48,2304]{3,1,0,2:T(4,128)}, u32[]{:S(2)}, u32[]{:S(2)}) async-start(f32[1,4,48,2304]{3,1,0,2:T(4,128)} %copy.181), calls=%async_computation.7 | async-start | bytes 3538944 | tf_op jit(solution)/shard_map/all_to_all | solution.py:67
  491.4 4.1 collective-permute-start.2
  495.5 179.3 %collective-permute-start.4 = (f32[4]{0:T(128)S(1)}, f32[4]{0:T(128)S(1)}, u32[]{:S(2)}, u32[]{:S(2)}) collective-permute-start(f32[4]{0:T(128)S(1)} %collective-permute-done.2), channel_id=1, source_target_pairs={{28,0},{0,4},{4,8},{8,12},{12,16},{16,20},{20,24},{24,28},{29,1},{... | collective-permute-start | bytes 56 | tf_op jit(solution)/shard_map/ppermute | solution.py:16
  579.8 4.9 copy-start.16
  579.8 5.8 copy-start.1
  579.8 90.1 %all-to-all-start.1 = ((f32[1,4,48,2304]{3,1,0,2:T(4,128)}), f32[1,4,48,2304]{3,1,0,2:T(4,128)}, u32[]{:S(2)}, u32[]{:S(2)}) async-start(f32[1,4,48,2304]{3,1,0,2:T(4,128)} %copy.151), calls=%async_computation.1 | async-start | bytes 3538944 | tf_op jit(solution)/shard_map/all_to_all | solution.py:67
  669.9 4.7 copy-start.13
  669.9 40.8 %all-to-all-start.9 = ((f32[1,4,48,2304]{3,1,0,2:T(4,128)}), f32[1,4,48,2304]{3,1,0,2:T(4,128)S(1)}, u32[]{:S(2)}, u32[]{:S(2)}) async-start(f32[1,4,48,2304]{3,1,0,2:T(4,128)} %copy.191), calls=%async_computation.9 | async-start | bytes 3538944 | tf_op jit(solution)/shard_map/all_to_all | solution.py:67
  676.0 18.1 %copy-start.11 = (f32[4,12,2304]{2,0,1:T(4,128)S(1)}, f32[4,12,2304]{2,0,1:T(4,128)}, u32[]{:S(2)}) copy-start(f32[4,12,2304]{2,0,1:T(4,128)} %copy-done.10) | copy-start | bytes 1327108
  683.7 6.8 collective-permute-start.8
  685.2 8.8 %collective-permute-start.6 = (f32[4]{0:T(128)S(1)}, f32[4]{0:T(128)S(1)}, u32[]{:S(2)}, u32[]{:S(2)}) collective-permute-start(f32[4]{0:T(128)S(1)} %collective-permute-done.4), channel_id=1, source_target_pairs={{28,0},{0,4},{4,8},{8,12},{12,16},{16,20},{20,24},{24,28},{29,1},{... | collective-permute-start | bytes 56 | tf_op jit(solution)/shard_map/ppermute | solution.py:16
  690.6 8.7 %collective-permute-start.9 = (f32[4,12,2304]{2,0,1:T(4,128)S(1)}, f32[4,12,2304]{2,0,1:T(4,128)S(1)}, u32[]{:S(2)}, u32[]{:S(2)}) collective-permute-start(f32[4,12,2304]{2,0,1:T(4,128)S(1)} %add.170), channel_id=1, source_target_pairs={{28,0},{0,4},{4,8},{8,12},{12,16},{16,20},{20,24},{24,28},{29,1},{... | collective-permute-start | bytes 1327112 | tf_op jit(solution)/shard_map/ppermute | solution.py:16
  700.2 13.6 %collective-permute-start.10 = (f32[4,12,2304]{2,0,1:T(4,128)}, f32[4,12,2304]{2,0,1:T(4,128)}, u32[]{:S(2)}, u32[]{:S(2)}) collective-permute-start(f32[4,12,2304]{2,0,1:T(4,128)} %add.171), channel_id=1, source_target_pairs={{12,0},{16,4},{20,8},{24,12},{28,16},{0,20},{4,24},{8,28},{13,1},{... | collective-permute-start | bytes 1327112 | tf_op jit(solution)/shard_map/ppermute | solution.py:16
  707.5 6.2 copy-start.6
  707.5 6.2 copy-start.7
  707.5 6.2 copy-start.8
  (5 other events, 11.5 us)
where the time goes:
time: 731 us; the launch traced here: 717 us
  local copies, waits for them, and re-layouts  278 us (38%)
  matrix products  159 us (22%)
  blocking collectives  132 us (18%)
  waiting for transfers between devices  60.7 us (8%)
  starting transfers between devices  60.5 us (8%)
  other arithmetic  25 us (3%)
    all_to_all x3, blocking collectives, solve_pairs(): lax.all_to_all(shaped, 'grid', split_axis=0, concat_axis=2, tiled=True)  132 us
    reshape x20, local copies, waits for them, and re-layouts, apply_transform(): first.reshape(batch_size * extent, extent, extent)  105 us
    dot_general x10, matrix products, apply_transform(): jnp.matmul(second.reshape(batch_size * extent * extent, extent), matrix.T...  92.3 us
    reshape x10, local copies, waits for them, and re-layouts, apply_transform(): second.reshape(batch_size * extent * extent, extent)  50.9 us
    transpose x10, local copies, waits for them, and re-layouts, apply_transform(): jnp.matmul(matrix, first.reshape(batch_size * extent, extent, extent), pr...  50 us
    dot_general x10, matrix products, apply_transform(): jnp.matmul(matrix, first.reshape(batch_size * extent, extent, extent), pr...  36.4 us
    ppermute x11, waiting for transfers between devices, shifted(): return lax.ppermute(block, axis, route)  33.4 us
    another operation x10, local copies, waits for them, and re-layouts, solve_pairs(): screened_potential(fields, transform, kernel).reshape(pieces.shape)  32.8 us
  transfers between devices with their start and end apart: 18, of which 10 were waited for; matrix products, arithmetic and copies ran while one was open for 63% of the time, Pallas kernels for 0%

commit v1 on v0

v1 whole, which is shorter than its diff:
```python
import functools

import jax
import jax.numpy as jnp
import ml_dtypes
import numpy as np
from jax import lax
from jax.experimental import pallas as pl
from jax.experimental.pallas import tpu as pltpu
from jax.sharding import PartitionSpec as P

screen_alpha = 2.0
screen_scale = 4.0


def split_halves(table):
    high = table.astype(ml_dtypes.bfloat16)
    low = (table - high.astype(np.float64)).astype(ml_dtypes.bfloat16)
    return high, low


@functools.cache
def transform_tables(extent):
    half = extent // 2
    position = np.arange(extent)
    angles = 2.0 * np.pi / extent * (position[:, None] * position[None, :] % extent)
    cas = np.cos(angles) + np.sin(angles)
    planes = [split_halves(np.kron(cas[:half, e::2], cas)) for e in (0, 1)]
    plane_tables = np.stack([np.stack(p) for p in planes])
    high, low = split_halves(cas)
    line_table = np.concatenate([high, high, low], axis=1)
    signed = np.where(position <= half, position, position - extent) ** 2
    order = np.concatenate([position[0::2], position[1::2]])
    shells = signed[:, None, None] + signed[order][None, :, None] + signed[None, None, :]
    shells = shells.reshape(extent, extent * extent).astype(np.int32)
    ratios = shells / screen_alpha
    screen = np.where(shells > 0, (1.0 - np.exp(-ratios)) / np.maximum(ratios, 0.1), 1.0)
    screen = (screen * (screen_scale / extent**3)).astype(np.float32)
    return plane_tables, line_table, shells, screen


@functools.cache
def pair_lists(bands, grids, count):
    chips = bands // 2
    parts = max(1, grids // chips)
    assert chips * parts == grids and count % parts == 0
    visitors = count // parts
    lists = []
    for g in range(grids):
        kind, part = divmod(g, parts)
        for core in range(2):
            pairs = []
            if kind == 0:
                own = [(i, j) for i in range(count) for j in range(i, count)]
                pairs += own[part::parts]
                for i in range(count):
                    for j in range(visitors):
                        if (i + j + part * visitors) % 2 == core:
                            pairs.append((i, count + j))
            else:
                pairs += [(i, count + j) for j in range(visitors) for i in range(count)]
            lists.append(pairs)
    longest = max(map(len, lists))
    batch = max(d for d in range(1, 10) if longest % d == 0)
    table = np.zeros((len(lists), longest, 4), np.int32)
    for row, pairs in enumerate(lists):
        for k, (a, b) in enumerate(pairs):
            table[row, k] = (a, b, 1, int(a != b))
    return table.reshape(grids, 2, longest * 4), longest, batch, parts, visitors


def routes(bands, grids, parts):
    moves = []
    for b in range(bands):
        for g in range(grids):
            chip, core = divmod(b, 2)
            other = chip ^ (g // parts)
            flip = 1 if other <= chip else 0
            source = other * 2 + (core ^ flip)
            moves.append((source * grids + g, b * grids + g))
    return moves


def high_low(values):
    high = values.astype(jnp.bfloat16)
    low = (values - high.astype(jnp.float32)).astype(jnp.bfloat16)
    return high, low


def exchange_kernel(
    batch, longest, pairs, weights, cutoff, own, visiting, planes, line, shells, screen,
    out_own, out_visiting, fields, outs, high, low, work,
):
    count, extent, cells = own.shape
    visitors = visiting.shape[0]
    half = cells // 2
    fields[:count] = own[...]
    fields[count:] = visiting[...]
    outs[...] = jnp.zeros_like(outs)

    def run_batch(step, _):
        def form(p, _):
            k = (step * batch + p) * 4
            a, b = pairs[k], pairs[k + 1]
            rows = pl.ds(pl.multiple_of(p * extent, extent), extent)
            near = fields[a, :, :half] * fields[b, :, :half]
            far = fields[a, :, half:] * fields[b, :, half:]
            for e, folded in enumerate((near + far, near - far)):
                high[e, rows, :], low[e, rows, :] = high_low(folded)
            return 0

        lax.fori_loop(0, batch, form, 0)

        def forward(e, _):
            total = jnp.dot(low[e], planes[e, 0], preferred_element_type=jnp.float32)
            total += jnp.dot(high[e], planes[e, 1], preferred_element_type=jnp.float32)
            total += jnp.dot(high[e], planes[e, 0], preferred_element_type=jnp.float32)
            work[e] = total
            return 0

        lax.fori_loop(0, 2, forward, 0)

        def screened(p, _):
            rows = pl.ds(pl.multiple_of(p * extent, extent), extent)
            for e in range(2):
                lanes = pl.ds(e * half, half)
                h, l = high_low(work[e, rows, :])
                spectrum = jnp.dot(
                    line[...], jnp.concatenate([h, l, h], axis=0),
                    preferred_element_type=jnp.float32,
                )
                factor = jnp.where(shells[:, lanes] <= cutoff[0], screen[:, lanes], 0.0)
                h, l = high_low(spectrum * factor)
                back = jnp.dot(
                    line[...], jnp.concatenate([h, l, h], axis=0),
                    preferred_element_type=jnp.float32,
                )
                high[e, rows, :], low[e, rows, :] = high_low(back)
            return 0

        lax.fori_loop(0, batch, screened, 0)

        def inverse(e, _):
            def product(left, right):
                return lax.dot_general(
                    left, right, (((1,), (1,)), ((), ())), preferred_element_type=jnp.float32
                )

            total = product(low[e], planes[e, 0])
            total += product(high[e], planes[e, 1])
            total += product(high[e], planes[e, 0])
            work[e] = total
            return 0

        lax.fori_loop(0, 2, inverse, 0)

        def apply(p, _):
            k = (step * batch + p) * 4
            a, b = pairs[k], pairs[k + 1]
            rows = pl.ds(pl.multiple_of(p * extent, extent), extent)
            to_a = -weights[b] * pairs[k + 2].astype(jnp.float32)
            to_b = -weights[a] * pairs[k + 3].astype(jnp.float32)
            even, odd = work[0, rows, :], work[1, rows, :]
            for lanes, v in ((pl.ds(0, half), even + odd), (pl.ds(half, half), even - odd)):
                phi_a, phi_b = fields[a, :, lanes], fields[b, :, lanes]
                outs[a, :, lanes] = outs[a, :, lanes] + to_a * (phi_b * v)
                outs[b, :, lanes] = outs[b, :, lanes] + to_b * (phi_a * v)
            return 0

        lax.fori_loop(0, batch, apply, 0)
        return 0

    lax.fori_loop(0, longest // batch, run_batch, 0)
    out_own[...] = outs[:count]
    out_visiting[...] = outs[count:]


def on_device(bands, grids, orbitals, occupation, cutoff):
    count, thickness, cells = orbitals.shape
    extent = thickness * grids
    planes, line, shells, screen = transform_tables(extent)
    table, longest, batch, parts, visitors = pair_lists(bands, grids, count)
    moves = routes(bands, grids, parts)
    back = [(d, s) for s, d in moves]
    axes = ("band", "grid")
    g = lax.axis_index("grid")
    core = lax.axis_index("band") % 2
    first = g % parts * visitors

    weights = occupation.astype(jnp.float32) * 0.5
    own = lax.all_gather(orbitals, "grid", axis=1, tiled=True)
    sent = own if parts == 1 else lax.dynamic_slice_in_dim(own, first, visitors, 0)
    sent_weights = weights if parts == 1 else lax.dynamic_slice_in_dim(weights, first, visitors, 0)
    visiting = lax.ppermute(sent, axes, moves)
    visiting_weights = lax.ppermute(sent_weights, axes, moves)
    all_weights = jnp.concatenate([weights, visiting_weights])
    pairs = jnp.asarray(table)[g, core]

    rows = batch * extent
    smem = pl.BlockSpec(memory_space=pltpu.SMEM)
    vmem = pl.BlockSpec(memory_space=pltpu.VMEM)
    slots = count + visitors
    out_own, out_visiting = pl.pallas_call(
        functools.partial(exchange_kernel, batch, longest),
        out_shape=(
            jax.ShapeDtypeStruct(own.shape, jnp.float32),
            jax.ShapeDtypeStruct(visiting.shape, jnp.float32),
        ),
        in_specs=[smem] * 3 + [vmem] * 6,
        out_specs=(vmem, vmem),
        scratch_shapes=[
            pltpu.VMEM((slots, extent, cells), jnp.float32),
            pltpu.VMEM((slots, extent, cells), jnp.float32),
            pltpu.VMEM((2, rows, cells // 2), jnp.bfloat16),
            pltpu.VMEM((2, rows, cells // 2), jnp.bfloat16),
            pltpu.VMEM((2, rows, cells // 2), jnp.float32),
        ],
        compiler_params=pltpu.CompilerParams(vmem_limit_bytes=56 * 1024 * 1024),
    )(
        pairs, all_weights, cutoff.reshape(1), own, visiting,
        jnp.asarray(planes), jnp.asarray(line), jnp.asarray(shells), jnp.asarray(screen),
    )
    returned = lax.ppermute(out_visiting, axes, back)
    if parts == 1:
        total = out_own + returned
    else:
        near = lax.dynamic_slice_in_dim(out_own, first, visitors, 0) + returned
        total = lax.dynamic_update_slice_in_dim(out_own, near, first, 0)
    return lax.psum_scatter(total, "grid", scatter_dimension=1, tiled=True)


def solution(mesh):
    placed = (P("band", "grid", None), P("band"), P())
    return jax.shard_map(
        functools.partial(on_device, mesh.shape["band"], mesh.shape["grid"]),
        mesh=mesh, in_specs=placed, out_specs=P("band", "grid", None), check_vma=False,
    )
```

time: 731 us -> 285 us (0.39); the launches traced: 717 us -> 282 us
  local copies, waits for them, and re-layouts: 278 us -> 9.59 us
  matrix products: 159 us -> 0 us
  waiting for transfers between devices: 60.7 us -> 194 us
  blocking collectives: 132 us -> 0 us
  Pallas kernels: 0 us -> 58.8 us
  starting transfers between devices: 60.5 us -> 2.6 us
  other arithmetic: 25 us -> 2.44 us
  between operations: 1.55 us -> 14.7 us
    reshape x35 -> x0, local copies, waits for them, and re-layouts: 179 us -> none  [the longest x20 105 us: apply_transform(): first.reshape(batch_size * extent, extent, extent)]
    dot_general x30 -> x0, matrix products: 159 us -> none  [the longest x10 92.3 us: apply_transform(): jnp.matmul(second.reshape(batch_size * extent * extent, extent), matrix.T...]
    all_to_all x3 -> x0, blocking collectives: 132 us -> none  [solve_pairs(): lax.all_to_all(shaped, 'grid', split_axis=0, concat_axis=2, tiled=True)]
    unnamed x0 -> x3, waiting for transfers between devices: none -> 76.2 us
    pallas_call x0 -> x1, Pallas kernels: none -> 58.8 us  [on_device(): pl.pallas_call(functools.partial(exchange_kernel, batch, longest), out_sh...]
    transpose x10 -> x0, local copies, waits for them, and re-layouts: 50 us -> none  [apply_transform(): jnp.matmul(matrix, first.reshape(batch_size * extent, extent, extent), pr...]
    ppermute x11 -> x3, waiting for transfers between devices: 33.4 us -> 76.3 us  [the longest x1 39.4 us: on_device(): returned = lax.ppermute(out_visiting, axes, back)]
    all_gather x0 -> x1, waiting for transfers between devices: none -> 41.7 us  [on_device(): own = lax.all_gather(orbitals, 'grid', axis=1, tiled=True)]
  transfers between devices with their start and end apart: 18 -> 5, of which waited for: 10 -> 4; matrix products, arithmetic and copies ran while one was open for 63% -> 1% of each run, Pallas kernels for 0% -> 0%
where the time goes in v1:
time: 285 us; the launch traced here: 282 us
  waiting for transfers between devices  194 us (68%)
  Pallas kernels  58.8 us (21%)
  between operations  14.7 us (5%)
  local copies, waits for them, and re-layouts  9.59 us (3%)
    unnamed x3, waiting for transfers between devices  76.2 us
    pallas_call x1, Pallas kernels, on_device(): pl.pallas_call(functools.partial(exchange_kernel, batch, longest), out_sh...  58.8 us
    all_gather x1, waiting for transfers between devices, on_device(): own = lax.all_gather(orbitals, 'grid', axis=1, tiled=True)  41.7 us
    ppermute x1, waiting for transfers between devices, on_device(): returned = lax.ppermute(out_visiting, axes, back)  39.4 us
    ppermute x1, waiting for transfers between devices, on_device(): visiting_weights = lax.ppermute(sent_weights, axes, moves)  36.9 us
  transfers between devices with their start and end apart: 5, of which 4 were waited for; matrix products, arithmetic and copies ran while one was open for 1% of the time, Pallas kernels for 0%

profile of v1, /device:TPU:11, one launch (start us, length us, event | category | flops | bytes accessed | tf_op | source)
XLA Modules:
  0.0 282.4 jit_solution(18417686958492769616)
XLA Ops:
  6.5 0.0 all-gather.2.cloned.1.call-start
  6.5 0.7 all-gather.2.cloned.1.call-update
  7.3 0.0 copy-start.2
  7.3 0.0 all-reduce.3.cloned.1.call-start
  7.3 41.7 %all-gather.2.cloned.1.call-done = f32[4,48,2304]{2,0,1:T(4,128)} async-done(((f32[4,12,2304]{2,0,1:T(4,128)}), f32[4,48,2304]{2,0,1:T(4,128)}) %all-gather.2.cloned.1.call-update) | async-done | bytes 1769488 | tf_op jit(solution)/shard_map/all_gather | solution.py:191
  49.1 1.8 copy.12.own
  50.9 0.0 copy-start
  50.9 0.3 collective-permute-start.1
  51.2 0.0 copy-done.2
  51.2 2.0 collective-permute-start
  53.8 1.2 dynamic-slice_bitcast_fusion.pairs
  55.0 36.9 %collective-permute-done = f32[4]{0:T(128)S(1)} collective-permute-done((f32[4]{0:T(128)S(1)}, f32[4]{0:T(128)S(1)}, u32[]{:S(2)}, u32[]{:S(2)}) %collective-permute-start) | collective-permute-done | bytes 48 | tf_op jit(solution)/shard_map/ppermute | solution.py:195
  91.9 0.6 pad_maximum_fusion.weights
  92.6 0.0 collective-permute-done.1.visiting
  92.6 0.0 copy-start.1
  92.6 0.0 copy-done
  92.6 1.2 copy-done.1
  93.8 58.8 %shard_map.82 = (f32[4,48,2304]{2,1,0:T(8,128)}, f32[4,48,2304]{2,1,0:T(8,128)}) custom-call(s32[72]{0:T(128)} %dynamic-slice_bitcast_fusion.pairs, f32[8]{0:T(128)} %pad_maximum_fusion.weights, s32[1]{0:T(128)} %bitcast.4.cutoff, f32[4,48,2304]{2,1,0:T(8,128)} %copy-done, f32[4,48,2304]{2,1,0:T(8,128)} %copy-done.1, ...), custom_call_target="tpu_custom_call" | custom-call | tf_op jit(solution)/shard_map/pallas_call | solution.py:203
  152.6 0.3 collective-permute-start.2
  152.8 39.4 %collective-permute-done.2 = f32[4,48,2304]{2,1,0:T(8,128)S(1)} collective-permute-done((f32[4,48,2304]{2,1,0:T(8,128)}, f32[4,48,2304]{2,1,0:T(8,128)S(1)}, u32[]{:S(2)}, u32[]{:S(2)}) %collective-permute-start.2) | collective-permute-done | bytes 1769504 | tf_op jit(solution)/shard_map/ppermute | solution.py:223
  192.3 1.8 add.18
  194.0 2.3 copy.13
  196.4 0.0 copy-start.3
  196.4 0.0 all-reduce.3.cloned.1.call-update
  196.4 0.6 copy-done.3
  197.1 0.6 dynamic-slice
  198.3 75.5 %all-reduce.3.cloned.1.call-done = f32[4,48,2304]{2,0,1:T(4,128)} async-done(((f32[4,48,2304]{2,0,1:T(4,128)}), f32[4,48,2304]{2,0,1:T(4,128)}) %all-reduce.3.cloned.1.call-update) | async-done | bytes 1769488
  273.8 1.8 constant_dynamic-slice_fusion
  (1 shorter events, 0.0 us)
Async XLA Ops:
  6.5 42.5 %all-gather.2.cloned.1.call-start = ((), (), s32[]{:S(2)}) async-start(), calls=%async_computation | async-start | bytes 2211840 | tf_op jit(solution)/shard_map/all_gather | solution.py:191
  7.3 44.0 %copy-start.2 = (s32[4]{0:T(128)S(1)}, s32[4]{0:T(128)}, u32[]{:S(2)}) copy-start(s32[4]{0:T(128)} %param.9) | copy-start | bytes 52
  7.3 266.5 %all-reduce.3.cloned.1.call-start = ((), (), s32[]{:S(2)}) async-start(), calls=%async_computation.1 | async-start | bytes 3538944
  50.9 41.7 %copy-start = (f32[4,48,2304]{2,1,0:T(8,128)}, f32[4,48,2304]{2,1,0:T(8,128)S(1)}, u32[]{:S(2)}) copy-start(f32[4,48,2304]{2,1,0:T(8,128)S(1)} %copy.12.own) | copy-start | bytes 5308420
  50.9 41.7 %collective-permute-start.1 = (f32[4,48,2304]{2,1,0:T(8,128)S(1)}, f32[4,48,2304]{2,1,0:T(8,128)S(1)}, u32[]{:S(2)}, u32[]{:S(2)}) collective-permute-start(f32[4,48,2304]{2,1,0:T(8,128)S(1)} %copy.12.own), channel_id=1, source_target_pairs={{4,0},{9,1},{18,2},{27,3},{0,4},{13,5},{22,6},{31,7},{12,8},{5,9},... | collective-permute-start | bytes 5308424 | tf_op jit(solution)/shard_map/ppermute | solution.py:194
  51.2 40.7 %collective-permute-start = (f32[4]{0:T(128)S(1)}, f32[4]{0:T(128)S(1)}, u32[]{:S(2)}, u32[]{:S(2)}) collective-permute-start(f32[4]{0:T(128)S(1)} %convert_multiply_fusion), channel_id=1, source_target_pairs={{4,0},{9,1},{18,2},{27,3},{0,4},{13,5},{22,6},{31,7},{12,8},{5,9},... | collective-permute-start | bytes 56 | tf_op jit(solution)/shard_map/ppermute | solution.py:195
  92.6 1.2 copy-start.1
  152.6 39.7 %collective-permute-start.2 = (f32[4,48,2304]{2,1,0:T(8,128)}, f32[4,48,2304]{2,1,0:T(8,128)S(1)}, u32[]{:S(2)}, u32[]{:S(2)}) collective-permute-start(f32[4,48,2304]{2,1,0:T(8,128)} %get-tuple-element.8), channel_id=1, source_target_pairs={{0,4},{1,9},{2,18},{3,27},{4,0},{5,13},{6,22},{7,31},{8,12},{9,5},... | collective-permute-start | bytes 5308424 | tf_op jit(solution)/shard_map/ppermute | solution.py:223
  196.4 0.7 copy-start.3
Sparse Core Ops, SparseCore 0:
  8.9 40.0 all-gather.1
  196.5 77.1 all-reduce.2

commit v2 on v1

--- a/solution.py
+++ b/solution.py
@@ -54,11 +54,12 @@
                 own = [(i, j) for i in range(count) for j in range(i, count)]
                 pairs += own[part::parts]
                 for i in range(count):
-                    for j in range(visitors):
-                        if (i + j + part * visitors) % 2 == core:
+                    for j in range(part * visitors, part * visitors + visitors):
+                        if (i + j) % 2 == core:
                             pairs.append((i, count + j))
             else:
-                pairs += [(i, count + j) for j in range(visitors) for i in range(count)]
+                kept = range(part * visitors, part * visitors + visitors)
+                pairs += [(i, count + j) for j in kept for i in range(count)]
             lists.append(pairs)
     longest = max(map(len, lists))
     batch = max(d for d in range(1, 10) if longest % d == 0)
@@ -66,19 +67,195 @@
     for row, pairs in enumerate(lists):
         for k, (a, b) in enumerate(pairs):
             table[row, k] = (a, b, 1, int(a != b))
-    return table.reshape(grids, 2, longest * 4), longest, batch, parts, visitors
-
-
-def routes(bands, grids, parts):
-    moves = []
-    for b in range(bands):
-        for g in range(grids):
-            chip, core = divmod(b, 2)
-            other = chip ^ (g // parts)
-            flip = 1 if other <= chip else 0
-            source = other * 2 + (core ^ flip)
-            moves.append((source * grids + g, b * grids + g))
-    return moves
+    return table.reshape(grids, 2, longest * 4), longest, batch, parts
+
+
+def partners(bands, parts):
+    band, g = lax.axis_index("band"), lax.axis_index("grid")
+    chip, core, kind = band // 2, band % 2, g // parts
+    other = 0
+    bit = 1
+    while bit < bands // 2:
+        other += (chip // bit % 2 + kind // bit % 2) % 2 * bit
+        bit *= 2
+    source_flip = jnp.where(other <= chip, 1, 0)
+    target_flip = jnp.where(chip <= other, 1, 0)
+    return other * 2 + (core + source_flip) % 2, other * 2 + (core + target_flip) % 2
+
+
+MESH = pl.DeviceIdType.MESH
+
+
+def greet(z, grids, source, target):
+    barrier = pltpu.get_barrier_semaphore()
+
+    @pl.when(z > 0)
+    def _():
+        pl.semaphore_signal(barrier, inc=1, device_id={"grid": z - 1}, device_id_type=MESH)
+
+    @pl.when(z < grids - 1)
+    def _():
+        pl.semaphore_signal(barrier, inc=1, device_id={"grid": z + 1}, device_id_type=MESH)
+
+    pl.semaphore_signal(barrier, inc=1, device_id={"band": source}, device_id_type=MESH)
+    pl.semaphore_signal(barrier, inc=1, device_id={"band": target}, device_id_type=MESH)
+    pl.semaphore_wait(barrier, 2 + jnp.where(z > 0, 1, 0) + jnp.where(z < grids - 1, 1, 0))
+
+
+def gather_kernel(
+    bands, grids, parts, slab, own, visiting,
+    local_sem, up_send, down_send, z_recv, visit_send, visit_recv,
+):
+    thickness = slab.shape[0]
+    z = lax.axis_index("grid")
+    source, target = partners(bands, parts)
+    greet(z, grids, source, target)
+
+    def part(ref, t):
+        return ref.at[pl.ds(t * thickness, thickness)]
+
+    def along(t, step, send, to):
+        from_ref = slab if step == 0 else part(own, t)
+        return pltpu.make_async_remote_copy(
+            src_ref=from_ref, dst_ref=part(own, t), send_sem=send.at[step],
+            recv_sem=z_recv.at[t], device_id={"grid": to}, device_id_type=MESH,
+        )
+
+    def visit(t, mine):
+        return pltpu.make_async_remote_copy(
+            src_ref=slab if mine else part(own, t), dst_ref=part(visiting, t),
+            send_sem=visit_send.at[t], recv_sem=visit_recv.at[t],
+            device_id={"band": target}, device_id_type=MESH,
+        )
+
+    def climbs(step):
+        return (z >= step) & (z < grids - 1)
+
+    def falls(step):
+        return (z + step < grids) & (z > 0)
+
+    keep = pltpu.make_async_copy(slab, part(own, z), local_sem)
+    for step in range(grids):
+        below, above = z - step, z + step
+        if step > 0:
+            @pl.when(below >= 0)
+            def _():
+                along(below, step, up_send, z).wait_recv()
+
+            @pl.when(above < grids)
+            def _():
+                along(above, step, down_send, z).wait_recv()
+
+        if step < grids - 1:
+            @pl.when(climbs(step))
+            def _():
+                along(below, step, up_send, z + 1).start()
+
+            @pl.when(falls(step))
+            def _():
+                along(above, step, down_send, z - 1).start()
+
+        if step == 0:
+            visit(z, True).start()
+            keep.start()
+        else:
+            @pl.when(below >= 0)
+            def _():
+                visit(below, False).start()
+
+            @pl.when(above < grids)
+            def _():
+                visit(above, False).start()
+
+    for step in range(grids - 1):
+        @pl.when(climbs(step))
+        def _():
+            along(z - step, step, up_send, z + 1).wait_send()
+
+        @pl.when(falls(step))
+        def _():
+            along(z + step, step, down_send, z - 1).wait_send()
+
+    keep.wait()
+    for t in range(grids):
+        visit(t, False).wait_send()
+        visit(t, False).wait_recv()
+
+
+def reduce_kernel(
+    bands, grids, parts, own, visiting, out, returned, up_in, down_in, up_out, down_out,
+    back_send, back_recv, up_send, up_recv, down_send, down_recv,
+):
+    thickness = out.shape[0]
+    z = lax.axis_index("grid")
+    source, target = partners(bands, parts)
+    greet(z, grids, source, target)
+
+    def rows(t):
+        return pl.ds(t * thickness, thickness)
+
+    def back(t):
+        return pltpu.make_async_remote_copy(
+            src_ref=visiting.at[rows(t)], dst_ref=returned.at[rows(t)],
+            send_sem=back_send.at[t], recv_sem=back_recv.at[t],
+            device_id={"band": source}, device_id_type=MESH,
+        )
+
+    def up(step):
+        return pltpu.make_async_remote_copy(
+            src_ref=up_out.at[step], dst_ref=up_in.at[step], send_sem=up_send.at[step],
+            recv_sem=up_recv.at[step], device_id={"grid": z + 1}, device_id_type=MESH,
+        )
+
+    def down(step):
+        return pltpu.make_async_remote_copy(
+            src_ref=down_out.at[step], dst_ref=down_in.at[step], send_sem=down_send.at[step],
+            recv_sem=down_recv.at[step], device_id={"grid": z - 1}, device_id_type=MESH,
+        )
+
+    for o in range(grids):
+        back(jnp.where(z < grids // 2, grids - 1 - o, o)).start()
+    last = grids - 1
+    for step in range(grids - 1):
+        for copy, inbox, outbox, z_from, t in (
+            (up, up_in, up_out, z, last - step + z),
+            (down, down_in, down_out, last - z, step - last + z),
+        ):
+            @pl.when(z_from <= step)
+            def _():
+                back(t).wait_recv()
+                outbox[step] = own[rows(t)] + returned[rows(t)]
+                if step > 0:
+                    @pl.when(z_from >= 1)
+                    def _():
+                        copy(step - 1).wait_recv()
+                        outbox[step] = outbox[step] + inbox[step - 1]
+                copy(step).start()
+
+    back(z).wait_recv()
+    out[...] = own[rows(z)] + returned[rows(z)]
+
+    @pl.when(z >= 1)
+    def _():
+        up(last - 1).wait_recv()
+        out[...] = out[...] + up_in[last - 1]
+
+    @pl.when(z < last)
+    def _():
+        down(last - 1).wait_recv()
+        out[...] = out[...] + down_in[last - 1]
+
+    for step in range(grids - 1):
+        @pl.when(z <= step)
+        def _():
+            up(step).wait_send()
+
+        @pl.when(last - z <= step)
+        def _():
+            down(step).wait_send()
+
+    for t in range(grids):
+        back(t).wait_send()
 
 
 def high_low(values):
@@ -179,27 +356,34 @@
     count, thickness, cells = orbitals.shape
     extent = thickness * grids
     planes, line, shells, screen = transform_tables(extent)
-    table, longest, batch, parts, visitors = pair_lists(bands, grids, count)
-    moves = routes(bands, grids, parts)
-    back = [(d, s) for s, d in moves]
-    axes = ("band", "grid")
+    table, longest, batch, parts = pair_lists(bands, grids, count)
     g = lax.axis_index("grid")
-    core = lax.axis_index("band") % 2
-    first = g % parts * visitors
-
+    band = lax.axis_index("band")
     weights = occupation.astype(jnp.float32) * 0.5
-    own = lax.all_gather(orbitals, "grid", axis=1, tiled=True)
-    sent = own if parts == 1 else lax.dynamic_slice_in_dim(own, first, visitors, 0)
-    sent_weights = weights if parts == 1 else lax.dynamic_slice_in_dim(weights, first, visitors, 0)
-    visiting = lax.ppermute(sent, axes, moves)
-    visiting_weights = lax.ppermute(sent_weights, axes, moves)
-    all_weights = jnp.concatenate([weights, visiting_weights])
-    pairs = jnp.asarray(table)[g, core]
+    every_weight = lax.all_gather(weights, "band", axis=0)
+    source, _ = partners(bands, parts)
+    all_weights = jnp.concatenate([weights, every_weight[source]])
+    pairs = jnp.asarray(table)[g, band % 2]
+
+    anywhere = pl.BlockSpec(memory_space=pl.ANY)
+    dma = pltpu.SemaphoreType.DMA
+    whole = jax.ShapeDtypeStruct((extent, count, cells), jnp.float32)
+    gathered = pl.pallas_call(
+        functools.partial(gather_kernel, bands, grids, parts),
+        out_shape=(whole, whole),
+        in_specs=[anywhere],
+        out_specs=(anywhere, anywhere),
+        scratch_shapes=[
+            dma, dma((grids,)), dma((grids,)), dma((grids,)), dma((grids,)), dma((grids,)),
+        ],
+        compiler_params=pltpu.CompilerParams(collective_id=0, has_side_effects=True),
+    )(orbitals.transpose(1, 0, 2))
+    own, visiting = (x.transpose(1, 0, 2) for x in gathered)
 
     rows = batch * extent
     smem = pl.BlockSpec(memory_space=pltpu.SMEM)
     vmem = pl.BlockSpec(memory_space=pltpu.VMEM)
-    slots = count + visitors
+    slots = 2 * count
     out_own, out_visiting = pl.pallas_call(
         functools.partial(exchange_kernel, batch, longest),
         out_shape=(
@@ -220,13 +404,22 @@
         pairs, all_weights, cutoff.reshape(1), own, visiting,
         jnp.asarray(planes), jnp.asarray(line), jnp.asarray(shells), jnp.asarray(screen),
     )
-    returned = lax.ppermute(out_visiting, axes, back)
-    if parts == 1:
-        total = out_own + returned
-    else:
-        near = lax.dynamic_slice_in_dim(out_own, first, visitors, 0) + returned
-        total = lax.dynamic_update_slice_in_dim(out_own, near, first, 0)
-    return lax.psum_scatter(total, "grid", scatter_dimension=1, tiled=True)
+    steps = grids - 1
+    slabs = pltpu.VMEM((steps, thickness, count, cells), jnp.float32)
+    total = pl.pallas_call(
+        functools.partial(reduce_kernel, bands, grids, parts),
+        out_shape=jax.ShapeDtypeStruct((thickness, count, cells), jnp.float32),
+        in_specs=[vmem, vmem],
+        out_specs=vmem,
+        scratch_shapes=[
+            pltpu.VMEM((extent, count, cells), jnp.float32), slabs, slabs, slabs, slabs,
+            dma((grids,)), dma((grids,)), dma((steps,)), dma((steps,)), dma((steps,)), dma((steps,)),
+        ],
+        compiler_params=pltpu.CompilerParams(
+            collective_id=1, has_side_effects=True, vmem_limit_bytes=56 * 1024 * 1024
+        ),
+    )(out_own.transpose(1, 0, 2), out_visiting.transpose(1, 0, 2))
+    return total.transpose(1, 0, 2)
 
 
 def solution(mesh):

time: 285 us -> 191 us (0.67)
  waiting for transfers between devices: 194 us -> 0 us
  Pallas kernels: 58.8 us -> 161 us
  between operations: 14.7 us -> 1.33 us
  blocking collectives: 0 us -> 11.2 us
  local copies, waits for them, and re-layouts: 9.59 us -> 15.1 us
    pallas_call x0 -> x2, Pallas kernels: none -> 103 us  [the longest x1 58.6 us: on_device(): pl.pallas_call(functools.partial(reduce_kernel, bands, grids, parts), out...]
    ppermute x3 -> x0, waiting for transfers between devices: 76.3 us -> none  [the longest x1 39.4 us: on_device(): returned = lax.ppermute(out_visiting, axes, back)]
    unnamed x3 -> x0, waiting for transfers between devices: 76.2 us -> none
    all_gather x1 -> x0, waiting for transfers between devices: 41.7 us -> none  [on_device(): own = lax.all_gather(orbitals, 'grid', axis=1, tiled=True)]
    unnamed x0 -> x1, blocking collectives: none -> 11.2 us
    pallas_call x0 -> x2, local copies, waits for them, and re-layouts: none -> 6.32 us  [on_device(): pl.pallas_call(functools.partial(exchange_kernel, batch, longest), out_sh...]
    transpose x0 -> x1, local copies, waits for them, and re-layouts: none -> 4.44 us  [on_device(): own, visiting = (x.transpose(1, 0, 2) for x in gathered)]
  transfers between devices with their start and end apart: 5 -> 0, of which waited for: 4 -> 0; matrix products, arithmetic and copies ran while one was open for 1% -> 0% of each run, Pallas kernels for 0% -> 0%
where the time goes in v2:
time: 191 us; the launch traced here: 190 us
  Pallas kernels  161 us (84%)
  local copies, waits for them, and re-layouts  15.1 us (8%)
  blocking collectives  11.2 us (6%)
    pallas_call x1, Pallas kernels, on_device(): pl.pallas_call(functools.partial(exchange_kernel, batch, longest), out_sh...  58.8 us
    pallas_call x1, Pallas kernels, on_device(): pl.pallas_call(functools.partial(reduce_kernel, bands, grids, parts), out...  58.6 us
    pallas_call x1, Pallas kernels, on_device(): pl.pallas_call(functools.partial(gather_kernel, bands, grids, parts), out...  44 us
    unnamed x1, blocking collectives  11.2 us
    pallas_call x2, local copies, waits for them, and re-layouts, on_device(): pl.pallas_call(functools.partial(exchange_kernel, batch, longest), out_sh...  6.32 us
    transpose x1, local copies, waits for them, and re-layouts, on_device(): own, visiting = (x.transpose(1, 0, 2) for x in gathered)  4.44 us

profile of v2, /device:TPU:11, one launch (start us, length us, event | category | flops | bytes accessed | tf_op | source)
XLA Modules:
  0.0 190.5 jit_solution(4710174303478792541)
XLA Ops:
  0.7 1.2 dynamic-slice
  2.5 1.2 dynamic-slice_bitcast_fusion.1.pairs
  3.8 0.7 convert_multiply_fusion
  4.5 0.1 reshape.4
  4.6 11.2 %all-reduce.1 = f32[8,4]{1,0:T(8,128)S(1)} all-reduce(f32[8,4]{1,0:T(8,128)S(1)} %reshape.4), channel_id=2, replica_groups=mesh['band'=8,'grid'=4] {'band'}, use_global_device_ids=true, to_apply=%add | all-reduce | flops 32 | bytes 256
  15.8 0.7 pad_maximum_fusion.weights
  16.5 44.0 %shard_map.82 = (f32[48,4,2304]{2,1,0:T(4,128)}, f32[48,4,2304]{2,1,0:T(4,128)}) custom-call(f32[12,4,2304]{2,1,0:T(4,128)} %bitcast.22), custom_call_target="tpu_custom_call" | custom-call | tf_op jit(solution)/shard_map/pallas_call | solution.py:371
  60.5 4.4 %copy_bitcast_fusion.2 = (f32[4,48,2304]{2,1,0:T(8,128)}, f32[4,48,2304]{2,1,0:T(8,128)}) fusion(f32[48,4,2304]{2,1,0:T(4,128)} %get-tuple-element.10, f32[48,4,2304]{2,1,0:T(4,128)} %get-tuple-element.9), kind=kLoop, calls=%fused_computation.2 | loop fusion | bytes 7077888 | tf_op jit(solution)/shard_map/transpose | solution.py:381
  65.0 58.8 %shard_map.83 = (f32[4,48,2304]{2,1,0:T(8,128)}, f32[4,48,2304]{2,1,0:T(8,128)}) custom-call(s32[72]{0:T(128)} %dynamic-slice_bitcast_fusion.1.pairs, f32[8]{0:T(128)} %pad_maximum_fusion.weights, s32[1]{0:T(128)} %bitcast.18.cutoff, f32[4,48,2304]{2,1,0:T(8,128)} %get-tuple-element.16.own, f32[4,48,2304]{2,1,0:T(8,128)} %get-tuple-element.15.visiting, ...), custom_call_target="tpu_custom_call" | custom-call | tf_op jit(solution)/shard_map/pallas_call | solution.py:387
  123.8 0.0 copy-start
  123.8 4.0 %copy.22 = f32[4,48,2304]{2,0,1:T(4,128)} copy(f32[4,48,2304]{2,1,0:T(8,128)} %get-tuple-element.11) | data formatting | bytes 3538944 | tf_op jit(solution)/shard_map/pallas_call | solution.py:387
  127.8 0.0 copy-done
  127.8 2.3 %copy.21 = f32[4,48,2304]{2,0,1:T(4,128)} copy(f32[4,48,2304]{2,1,0:T(8,128)S(1)} %copy-done) | data formatting | bytes 3538944 | tf_op jit(solution)/shard_map/pallas_call | solution.py:387
  130.1 58.6 %shard_map.84 = f32[12,4,2304]{2,1,0:T(4,128)} custom-call(f32[48,4,2304]{2,1,0:T(4,128)} %bitcast.19, f32[48,4,2304]{2,1,0:T(4,128)} %bitcast.20), custom_call_target="tpu_custom_call" | custom-call | tf_op jit(solution)/shard_map/pallas_call | solution.py:409
  188.7 1.8 copy.26
  (2 shorter events, 0.0 us)
Async XLA Ops:
  123.8 4.0 %copy-start = (f32[4,48,2304]{2,1,0:T(8,128)S(1)}, f32[4,48,2304]{2,1,0:T(8,128)}, u32[]{:S(2)}) copy-start(f32[4,48,2304]{2,1,0:T(8,128)} %get-tuple-element.12) | copy-start | bytes 5308420

commit v3 on v2

--- a/solution.py
+++ b/solution.py
@@ -83,7 +83,19 @@
     return other * 2 + (core + source_flip) % 2, other * 2 + (core + target_flip) % 2
 
 
+def routes(bands, grids, parts):
+    moves = []
+    for b in range(bands):
+        for g in range(grids):
+            chip, core = divmod(b, 2)
+            other = chip ^ (g // parts)
+            source = other * 2 + (core ^ int(other <= chip))
+            moves.append((source * grids + g, b * grids + g))
+    return moves
+
+
 MESH = pl.DeviceIdType.MESH
+CHUNKS = 2
 
 
 def greet(z, grids, source, target):
@@ -191,71 +203,90 @@
     source, target = partners(bands, parts)
     greet(z, grids, source, target)
 
+    cells = out.shape[2] // CHUNKS
+    last = grids - 1
+
     def rows(t):
         return pl.ds(t * thickness, thickness)
 
-    def back(t):
+    def lanes(c):
+        return pl.ds(c * cells, cells)
+
+    def back(t, c):
         return pltpu.make_async_remote_copy(
-            src_ref=visiting.at[rows(t)], dst_ref=returned.at[rows(t)],
-            send_sem=back_send.at[t], recv_sem=back_recv.at[t],
+            src_ref=visiting.at[rows(t), :, lanes(c)], dst_ref=returned.at[rows(t), :, lanes(c)],
+            send_sem=back_send.at[t, c], recv_sem=back_recv.at[t, c],
             device_id={"band": source}, device_id_type=MESH,
         )
 
-    def up(step):
+    def up(step, c):
         return pltpu.make_async_remote_copy(
-            src_ref=up_out.at[step], dst_ref=up_in.at[step], send_sem=up_send.at[step],
-            recv_sem=up_recv.at[step], device_id={"grid": z + 1}, device_id_type=MESH,
+            src_ref=up_out.at[step, :, :, lanes(c)], dst_ref=up_in.at[step, :, :, lanes(c)],
+            send_sem=up_send.at[step, c], recv_sem=up_recv.at[step, c],
+            device_id={"grid": z + 1}, device_id_type=MESH,
         )
 
-    def down(step):
+    def down(step, c):
         return pltpu.make_async_remote_copy(
-            src_ref=down_out.at[step], dst_ref=down_in.at[step], send_sem=down_send.at[step],
-            recv_sem=down_recv.at[step], device_id={"grid": z - 1}, device_id_type=MESH,
+            src_ref=down_out.at[step, :, :, lanes(c)], dst_ref=down_in.at[step, :, :, lanes(c)],
+            send_sem=down_send.at[step, c], recv_sem=down_recv.at[step, c],
+            device_id={"grid": z - 1}, device_id_type=MESH,
         )
 
-    for o in range(grids):
-        back(jnp.where(z < grids // 2, grids - 1 - o, o)).start()
-    last = grids - 1
-    for step in range(grids - 1):
+    def turn(i):
+        o = i // CHUNKS
+        return back(jnp.where(z < grids // 2, last - o, o), i % CHUNKS)
+
+    turns = grids * CHUNKS
+    for i in range(min(2, turns)):
+        turn(i).start()
+    for i in range(turns):
+        turn(i).wait_send()
+        if i + 2 < turns:
+            turn(i + 2).start()
+        step, c = divmod(i, CHUNKS)
+        if step == last:
+            continue
         for copy, inbox, outbox, z_from, t in (
             (up, up_in, up_out, z, last - step + z),
             (down, down_in, down_out, last - z, step - last + z),
         ):
             @pl.when(z_from <= step)
             def _():
-                back(t).wait_recv()
-                outbox[step] = own[rows(t)] + returned[rows(t)]
+                back(t, c).wait_recv()
+                outbox[step, :, :, lanes(c)] = own[rows(t), :, lanes(c)] + returned[rows(t), :, lanes(c)]
                 if step > 0:
                     @pl.when(z_from >= 1)
                     def _():
-                        copy(step - 1).wait_recv()
-                        outbox[step] = outbox[step] + inbox[step - 1]
-                copy(step).start()
-
-    back(z).wait_recv()
-    out[...] = own[rows(z)] + returned[rows(z)]
-
-    @pl.when(z >= 1)
-    def _():
-        up(last - 1).wait_recv()
-        out[...] = out[...] + up_in[last - 1]
-
-    @pl.when(z < last)
-    def _():
-        down(last - 1).wait_recv()
-        out[...] = out[...] + down_in[last - 1]
+                        copy(step - 1, c).wait_recv()
+                        outbox[step, :, :, lanes(c)] = (
+                            outbox[step, :, :, lanes(c)] + inbox[step - 1, :, :, lanes(c)]
+                        )
+                copy(step, c).start()
+
+    for c in range(CHUNKS):
+        back(z, c).wait_recv()
+        out[:, :, lanes(c)] = own[rows(z), :, lanes(c)] + returned[rows(z), :, lanes(c)]
+
+        @pl.when(z >= 1)
+        def _():
+            up(last - 1, c).wait_recv()
+            out[:, :, lanes(c)] = out[:, :, lanes(c)] + up_in[last - 1, :, :, lanes(c)]
+
+        @pl.when(z < last)
+        def _():
+            down(last - 1, c).wait_recv()
+            out[:, :, lanes(c)] = out[:, :, lanes(c)] + down_in[last - 1, :, :, lanes(c)]
 
     for step in range(grids - 1):
-        @pl.when(z <= step)
-        def _():
-            up(step).wait_send()
-
-        @pl.when(last - z <= step)
-        def _():
-            down(step).wait_send()
-
-    for t in range(grids):
-        back(t).wait_send()
+        for c in range(CHUNKS):
+            @pl.when(z <= step)
+            def _():
+                up(step, c).wait_send()
+
+            @pl.when(last - z <= step)
+            def _():
+                down(step, c).wait_send()
 
 
 def high_low(values):
@@ -360,9 +391,8 @@
     g = lax.axis_index("grid")
     band = lax.axis_index("band")
     weights = occupation.astype(jnp.float32) * 0.5
-    every_weight = lax.all_gather(weights, "band", axis=0)
-    source, _ = partners(bands, parts)
-    all_weights = jnp.concatenate([weights, every_weight[source]])
+    visiting_weights = lax.ppermute(weights, ("band", "grid"), routes(bands, grids, parts))
+    all_weights = jnp.concatenate([weights, visiting_weights])
     pairs = jnp.asarray(table)[g, band % 2]
 
     anywhere = pl.BlockSpec(memory_space=pl.ANY)
@@ -413,7 +443,7 @@
         out_specs=vmem,
         scratch_shapes=[
             pltpu.VMEM((extent, count, cells), jnp.float32), slabs, slabs, slabs, slabs,
-            dma((grids,)), dma((grids,)), dma((steps,)), dma((steps,)), dma((steps,)), dma((steps,)),
+            *[dma((grids, CHUNKS))] * 2, *[dma((steps, CHUNKS))] * 4,
         ],
         compiler_params=pltpu.CompilerParams(
             collective_id=1, has_side_effects=True, vmem_limit_bytes=56 * 1024 * 1024

time: 191 us -> 174 us (0.911)
  blocking collectives: 11.2 us -> 0 us
  Pallas kernels: 161 us -> 157 us
    unnamed x1 -> x0, blocking collectives: 11.2 us -> none
    pallas_call x1, Pallas kernels: 58.6 us -> 51.7 us  [on_device(): pl.pallas_call(functools.partial(reduce_kernel, bands, grids, parts), out...]
    pallas_call x1, Pallas kernels: 44 us -> 46.1 us  [on_device(): pl.pallas_call(functools.partial(gather_kernel, bands, grids, parts), out...]
  transfers between devices with their start and end apart: 0 -> 1, of which waited for: 0 -> 0; matrix products, arithmetic and copies ran while one was open for 0% -> 3% of each run, Pallas kernels for 0% -> 27%
where the time goes in v3:
time: 174 us; the launch traced here: 173 us
  Pallas kernels  157 us (90%)
  local copies, waits for them, and re-layouts  13.8 us (8%)
    pallas_call x1, Pallas kernels, on_device(): pl.pallas_call(functools.partial(exchange_kernel, batch, longest), out_sh...  58.8 us
    pallas_call x1, Pallas kernels, on_device(): pl.pallas_call(functools.partial(reduce_kernel, bands, grids, parts), out...  51.7 us
    pallas_call x1, Pallas kernels, on_device(): pl.pallas_call(functools.partial(gather_kernel, bands, grids, parts), out...  46.1 us
    pallas_call x2, local copies, waits for them, and re-layouts, on_device(): pl.pallas_call(functools.partial(exchange_kernel, batch, longest), out_sh...  6.34 us
    transpose x1, local copies, waits for them, and re-layouts, on_device(): own, visiting = (x.transpose(1, 0, 2) for x in gathered)  4.45 us
  transfers between devices with their start and end apart: 1, of which 0 were waited for; matrix products, arithmetic and copies ran while one was open for 3% of the time, Pallas kernels for 27%

profile of v3, /device:TPU:11, one launch (start us, length us, event | category | flops | bytes accessed | tf_op | source)
XLA Modules:
  0.0 172.6 jit_solution(15472433771999828892)
XLA Ops:
  0.0 0.7 convert_multiply_fusion
  0.7 0.3 collective-permute-start
  1.6 46.1 %shard_map.82 = (f32[48,4,2304]{2,1,0:T(4,128)}, f32[48,4,2304]{2,1,0:T(4,128)}) custom-call(f32[12,4,2304]{2,1,0:T(4,128)} %bitcast.19), custom_call_target="tpu_custom_call" | custom-call | tf_op jit(solution)/shard_map/pallas_call | solution.py:401
  47.7 4.4 %copy_bitcast_fusion.2 = (f32[4,48,2304]{2,1,0:T(8,128)}, f32[4,48,2304]{2,1,0:T(8,128)}) fusion(f32[48,4,2304]{2,1,0:T(4,128)} %get-tuple-element.10, f32[48,4,2304]{2,1,0:T(4,128)} %get-tuple-element.9), kind=kLoop, calls=%fused_computation.2 | loop fusion | bytes 7077888 | tf_op jit(solution)/shard_map/transpose | solution.py:411
  52.1 1.2 dynamic-slice_bitcast_fusion.pairs
  53.3 0.0 collective-permute-done
  53.3 0.6 pad_maximum_fusion.weights
  53.9 58.8 %shard_map.83 = (f32[4,48,2304]{2,1,0:T(8,128)}, f32[4,48,2304]{2,1,0:T(8,128)}) custom-call(s32[72]{0:T(128)} %dynamic-slice_bitcast_fusion.pairs, f32[8]{0:T(128)} %pad_maximum_fusion.weights, s32[1]{0:T(128)} %bitcast.15.cutoff, f32[4,48,2304]{2,1,0:T(8,128)} %get-tuple-element.14.own, f32[4,48,2304]{2,1,0:T(8,128)} %get-tuple-element.13.visiting, ...), custom_call_target="tpu_custom_call" | custom-call | tf_op jit(solution)/shard_map/pallas_call | solution.py:417
  112.7 0.0 copy-start
  112.7 4.0 %copy.18 = f32[4,48,2304]{2,0,1:T(4,128)} copy(f32[4,48,2304]{2,1,0:T(8,128)} %get-tuple-element.11) | data formatting | bytes 3538944 | tf_op jit(solution)/shard_map/pallas_call | solution.py:417
  116.7 0.0 copy-done
  116.7 2.3 %copy.17 = f32[4,48,2304]{2,0,1:T(4,128)} copy(f32[4,48,2304]{2,1,0:T(8,128)S(1)} %copy-done) | data formatting | bytes 3538944 | tf_op jit(solution)/shard_map/pallas_call | solution.py:417
  119.1 51.7 %shard_map.84 = f32[12,4,2304]{2,1,0:T(4,128)} custom-call(f32[48,4,2304]{2,1,0:T(4,128)} %bitcast.16, f32[48,4,2304]{2,1,0:T(4,128)} %bitcast.17), custom_call_target="tpu_custom_call" | custom-call | tf_op jit(solution)/shard_map/pallas_call | solution.py:439
  170.8 1.8 %copy.21 = f32[4,12,2304]{2,0,1:T(4,128)} copy(f32[4,12,2304]{2,0,1:T(4,128)} %bitcast.18) | data formatting | bytes 884736
Async XLA Ops:
  0.7 52.7 %collective-permute-start = (f32[4]{0:T(128)S(1)}, f32[4]{0:T(128)S(1)}, u32[]{:S(2)}, u32[]{:S(2)}) collective-permute-start(f32[4]{0:T(128)S(1)} %convert_multiply_fusion), channel_id=1, source_target_pairs={{4,0},{9,1},{18,2},{27,3},{0,4},{13,5},{22,6},{31,7},{12,8},{5,9},... | collective-permute-start | bytes 56 | tf_op jit(solution)/shard_map/ppermute | solution.py:394
  112.7 4.0 %copy-start = (f32[4,48,2304]{2,1,0:T(8,128)S(1)}, f32[4,48,2304]{2,1,0:T(8,128)}, u32[]{:S(2)}) copy-start(f32[4,48,2304]{2,1,0:T(8,128)} %get-tuple-element.12) | copy-start | bytes 5308420

commit v4 on v3

--- a/solution.py
+++ b/solution.py
@@ -235,7 +235,8 @@
 
     def turn(i):
         o = i // CHUNKS
-        return back(jnp.where(z < grids // 2, last - o, o), i % CHUNKS)
+        t = jnp.where(z < grids // 2, (z + last - o) % grids, (z + 1 + o) % grids)
+        return back(t, i % CHUNKS)
 
     turns = grids * CHUNKS
     for i in range(min(2, turns)):

time: 174 us -> 167 us (0.960)
  Pallas kernels: 157 us -> 148 us
    pallas_call x1, Pallas kernels: 51.7 us -> 43.1 us  [on_device(): pl.pallas_call(functools.partial(reduce_kernel, bands, grids, parts), out...]
  transfers between devices with their start and end apart: 1 -> 1, of which waited for: 0 -> 0; matrix products, arithmetic and copies ran while one was open for 3% -> 3% of each run, Pallas kernels for 27% -> 28%
where the time goes in v4:
time: 167 us; the launch traced here: 164 us
  Pallas kernels  148 us (89%)
  local copies, waits for them, and re-layouts  13.8 us (8%)
    pallas_call x1, Pallas kernels, on_device(): pl.pallas_call(functools.partial(exchange_kernel, batch, longest), out_sh...  58.8 us
    pallas_call x1, Pallas kernels, on_device(): pl.pallas_call(functools.partial(gather_kernel, bands, grids, parts), out...  46.1 us
    pallas_call x1, Pallas kernels, on_device(): pl.pallas_call(functools.partial(reduce_kernel, bands, grids, parts), out...  43.1 us
    pallas_call x2, local copies, waits for them, and re-layouts, on_device(): pl.pallas_call(functools.partial(exchange_kernel, batch, longest), out_sh...  6.34 us
    transpose x1, local copies, waits for them, and re-layouts, on_device(): own, visiting = (x.transpose(1, 0, 2) for x in gathered)  4.45 us
  transfers between devices with their start and end apart: 1, of which 0 were waited for; matrix products, arithmetic and copies ran while one was open for 3% of the time, Pallas kernels for 28%

profile of v4, /device:TPU:11, one launch (start us, length us, event | category | flops | bytes accessed | tf_op | source)
XLA Modules:
  0.0 163.9 jit_solution(7358244301771658907)
XLA Ops:
  0.0 0.7 convert_multiply_fusion
  0.7 0.3 collective-permute-start
  1.6 46.1 %shard_map.82 = (f32[48,4,2304]{2,1,0:T(4,128)}, f32[48,4,2304]{2,1,0:T(4,128)}) custom-call(f32[12,4,2304]{2,1,0:T(4,128)} %bitcast.19), custom_call_target="tpu_custom_call" | custom-call | tf_op jit(solution)/shard_map/pallas_call | solution.py:402
  47.7 4.4 %copy_bitcast_fusion.2 = (f32[4,48,2304]{2,1,0:T(8,128)}, f32[4,48,2304]{2,1,0:T(8,128)}) fusion(f32[48,4,2304]{2,1,0:T(4,128)} %get-tuple-element.10, f32[48,4,2304]{2,1,0:T(4,128)} %get-tuple-element.9), kind=kLoop, calls=%fused_computation.2 | loop fusion | bytes 7077888 | tf_op jit(solution)/shard_map/transpose | solution.py:412
  52.1 1.2 dynamic-slice_bitcast_fusion.pairs
  53.3 0.0 collective-permute-done
  53.3 0.6 pad_maximum_fusion.weights
  53.9 58.8 %shard_map.83 = (f32[4,48,2304]{2,1,0:T(8,128)}, f32[4,48,2304]{2,1,0:T(8,128)}) custom-call(s32[72]{0:T(128)} %dynamic-slice_bitcast_fusion.pairs, f32[8]{0:T(128)} %pad_maximum_fusion.weights, s32[1]{0:T(128)} %bitcast.15.cutoff, f32[4,48,2304]{2,1,0:T(8,128)} %get-tuple-element.14.own, f32[4,48,2304]{2,1,0:T(8,128)} %get-tuple-element.13.visiting, ...), custom_call_target="tpu_custom_call" | custom-call | tf_op jit(solution)/shard_map/pallas_call | solution.py:418
  112.7 0.0 copy-start
  112.7 4.0 %copy.18 = f32[4,48,2304]{2,0,1:T(4,128)} copy(f32[4,48,2304]{2,1,0:T(8,128)} %get-tuple-element.11) | data formatting | bytes 3538944 | tf_op jit(solution)/shard_map/pallas_call | solution.py:418
  116.7 0.0 copy-done
  116.7 2.3 %copy.17 = f32[4,48,2304]{2,0,1:T(4,128)} copy(f32[4,48,2304]{2,1,0:T(8,128)S(1)} %copy-done) | data formatting | bytes 3538944 | tf_op jit(solution)/shard_map/pallas_call | solution.py:418
  119.1 43.1 %shard_map.84 = f32[12,4,2304]{2,1,0:T(4,128)} custom-call(f32[48,4,2304]{2,1,0:T(4,128)} %bitcast.16, f32[48,4,2304]{2,1,0:T(4,128)} %bitcast.17), custom_call_target="tpu_custom_call" | custom-call | tf_op jit(solution)/shard_map/pallas_call | solution.py:440
  162.1 1.8 %copy.21 = f32[4,12,2304]{2,0,1:T(4,128)} copy(f32[4,12,2304]{2,0,1:T(4,128)} %bitcast.18) | data formatting | bytes 884736
Async XLA Ops:
  0.7 52.7 %collective-permute-start = (f32[4]{0:T(128)S(1)}, f32[4]{0:T(128)S(1)}, u32[]{:S(2)}, u32[]{:S(2)}) collective-permute-start(f32[4]{0:T(128)S(1)} %convert_multiply_fusion), channel_id=1, source_target_pairs={{4,0},{9,1},{18,2},{27,3},{0,4},{13,5},{22,6},{31,7},{12,8},{5,9},... | collective-permute-start | bytes 56 | tf_op jit(solution)/shard_map/ppermute | solution.py:395
  112.7 4.0 %copy-start = (f32[4,48,2304]{2,1,0:T(8,128)S(1)}, f32[4,48,2304]{2,1,0:T(8,128)}, u32[]{:S(2)}) copy-start(f32[4,48,2304]{2,1,0:T(8,128)} %get-tuple-element.12) | copy-start | bytes 5308420
